TPU v7x, 32 devices: a whole 2x2x4 slice. The times are simulated.
32 devices in a mesh: pb: 8 (over z, x), ao: 4 (over y, core).
Axes of the slice: x: 2, y: 2, z: 4, core: 2. Of those that a mesh axis runs over, the one named last changes fastest.
Arguments:
- queries: bfloat16 [8192, 128], P('pb'), may hold values from -4 to 4
- centres: bfloat16 [8192, 128], P(('pb', 'ao')), may hold values from -4 to 4
- coefs: bfloat16 [8192, 4096], P('pb', 'ao'), may hold values from -3 to 3
- pattern: int32 [8, 5], replicated, may hold values from 0 to 1, as said below
Outputs:
- scores: bfloat16 [8192, 4096], P('pb', 'ao')
Inputs may be any that keep to these rules, and one draw needn't show every extreme that they name: pattern[i, j] tells whether query block i lists centre block i + j - 2; it is 0 where that block lies outside 0 to 7, and 1 for j = 2.
All inputs are finite; a program needn't handle non-finite values.
Results may differ from a plain program's by a relative error of at most 0.0049.
Values may be sent and summed in bfloat16 or wider, within the bound.
No kernel may reach another device: no remote copies, remote signals or barrier semaphores. Data moves between devices by JAX's collectives and lax.ppermute only.
A program may use at most 64 MiB of HBM per device.

v0:
```python
import math

import jax
import jax.numpy as jnp
from jax import lax
from jax.sharding import PartitionSpec as P

RADIUS_FACTOR = 1.3


def shifted(block, axis, distance):
    devices = range(lax.axis_size(axis))
    route = [(i - distance, i) for i in devices if i - distance in devices]
    return lax.ppermute(block, axis, route)


def query_norms(query_rows):
    query_wide = query_rows.astype(jnp.float32)
    return jnp.sum(query_wide * query_wide, axis=1)[:, None]


def wendland_block(query_rows, query_norm, centre_rows):
    centre_wide = centre_rows.astype(jnp.float32)
    centre_norm = jnp.sum(centre_wide * centre_wide, axis=1)[None, :]
    cross = jnp.dot(query_rows, centre_rows.T, preferred_element_type=jnp.float32)
    dist = jnp.sqrt(query_norm + centre_norm - 2.0 * cross)
    scaled = dist / (RADIUS_FACTOR * math.sqrt(query_rows.shape[1]))
    inner = jnp.maximum(1.0 - scaled, 0.0)
    return inner * inner * inner * inner * (4.0 * scaled + 1.0)


def contribute(query_rows, query_norm, centre_rows, coef_rows, weight):
    kern = (
        wendland_block(query_rows, query_norm, centre_rows) * weight.astype(jnp.float32)
    ).astype(jnp.bfloat16)
    return jnp.dot(kern, coef_rows, preferred_element_type=jnp.float32)


def per_device(queries, centres, coefs, pattern):
    band_width = pattern.shape[1]
    half_band = band_width // 2
    my_block = lax.axis_index("pb")
    my_pattern = lax.dynamic_index_in_dim(pattern, my_block, 0, keepdims=False)
    panel_coords = lax.all_gather(centres, "ao", axis=0, tiled=True)
    my_norm = query_norms(queries)
    offsets = [shift_by for shift_by in range(-half_band, half_band + 1) if shift_by != 0]
    accumulated = contribute(queries, my_norm, panel_coords, coefs, my_pattern[half_band])
    for shift_by in offsets:
        far_coords, far_coefs = shifted((panel_coords, coefs), "pb", -shift_by)
        accumulated = accumulated + contribute(
            queries, my_norm, far_coords, far_coefs, my_pattern[half_band + shift_by]
        )
    return accumulated.astype(jnp.bfloat16)


def solution(mesh):
    in_specs = (P("pb", None), P(("pb", "ao"), None), P("pb", "ao"), P())
    out_specs = P("pb", "ao")
    return jax.shard_map(
        per_device, mesh=mesh, in_specs=in_specs, out_specs=out_specs, check_vma=False
    )
```

profile of v0, /device:TPU:0, one launch (start us, length us, event | category | flops | bytes accessed | tf_op | source)
XLA Modules:
  0.0 166.5 jit_solution(13472319660385003156)
XLA Ops:
  0.0 0.0 copy-start
  0.0 6.4 %collective-permute-start.3 = (bf16[1024,1024]{1,0:T(8,128)(2,1)}, bf16[1024,1024]{1,0:T(8,128)(2,1)}, u32[]{:S(2)}, u32[]{:S(2)}) collective-permute-start(bf16[1024,1024]{1,0:T(8,128)(2,1)} %param.6), channel_id=1, source_target_pairs={{0,4},{4,8},{8,12},{12,16},{16,20},{20,24},{24,28},{1,5},{5,9},{9,... | collective-permute-start | bytes 6291464 | tf_op jit(solution)/shard_map/ppermute | solution.py:14
  6.4 6.0 %all_gather.3 = bf16[1024,128]{1,0:T(8,128)(2,1)S(1)} all-gather(bf16[256,128]{1,0:T(8,128)(2,1)} %param.5), channel_id=1, replica_groups=mesh['pb'=8,'ao'=4] {'ao'}, dimensions={0}, use_global_device_ids=true | all-gather | bytes 327680 | tf_op jit(solution)/shard_map/all_gather | solution.py:44
  12.4 1.3 collective-permute-start.6
  13.6 1.3 collective-permute-start.4
  14.9 4.6 %collective-permute-start.2 = (bf16[1024,128]{1,0:T(8,128)(2,1)S(1)}, bf16[1024,128]{1,0:T(8,128)(2,1)S(1)}, u32[]{:S(2)}, u32[]{:S(2)}) collective-permute-start(bf16[1024,128]{1,0:T(8,128)(2,1)S(1)} %all_gather.3), channel_id=1, source_target_pairs={{0,4},{4,8},{8,12},{12,16},{16,20},{20,24},{24,28},{1,5},{5,9},{9,... | collective-permute-start | bytes 786440 | tf_op jit(solution)/shard_map/ppermute | solution.py:14
  19.5 5.9 %collective-permute-start.1 = (bf16[1024,1024]{1,0:T(8,128)(2,1)}, bf16[1024,1024]{1,0:T(8,128)(2,1)}, u32[]{:S(2)}, u32[]{:S(2)}) collective-permute-start(bf16[1024,1024]{1,0:T(8,128)(2,1)} %param.6), channel_id=1, source_target_pairs={{0,8},{4,12},{8,16},{12,20},{16,24},{20,28},{1,9},{5,13},{9,17},{1... | collective-permute-start | bytes 6291464 | tf_op jit(solution)/shard_map/ppermute | solution.py:14
  25.4 0.0 copy-done
  25.4 0.7 fusion.45
  26.7 0.2 multiply_reduce_fusion.4
  27.0 1.2 multiply_reduce_fusion.5
  28.1 0.0 collective-permute-done.6
  28.1 1.3 collective-permute-start.5
  29.4 0.0 copy-start.1
  29.4 7.9 %fusion.19 = f32[1024,1024]{1,0:T(8,128)} fusion(bf16[1024,1024]{1,0:T(8,128)(2,1)} %param.6, bf16[1024,128]{1,0:T(8,128)(2,1)} %param.4, bf16[1024,128]{1,0:T(8,128)(2,1)S(1)} %all_gather.3, f32[]{:T(128)} %bitcast, f32[1024]{0:T(1024)S(1)} %multiply_reduce_fusion.4, f32[1024]{0:T(1024)S(1)} %multiply_reduce_fusion.5), kind=kOutput, calls=%fused_computation.25 | convolution fusion | flops 2430599168 | bytes 6823940 | tf_op jit(solution)/shard_map/dot_general | solution.py:36
  40.0 0.0 collective-permute-done.4
  40.1 26.7 %collective-permute-start = (bf16[1024,128]{1,0:T(8,128)(2,1)S(1)}, bf16[1024,128]{1,0:T(8,128)(2,1)S(1)}, u32[]{:S(2)}, u32[]{:S(2)}) collective-permute-start(bf16[1024,128]{1,0:T(8,128)(2,1)S(1)} %all_gather.3), channel_id=1, source_target_pairs={{0,8},{4,12},{8,16},{12,20},{16,24},{20,28},{1,9},{5,13},{9,17},{1... | collective-permute-start | bytes 786440 | tf_op jit(solution)/shard_map/ppermute | solution.py:14
  66.8 0.2 multiply_reduce_fusion
  67.0 0.2 multiply_reduce_fusion.1
  67.2 39.0 %collective-permute-done.2 = bf16[1024,128]{1,0:T(8,128)(2,1)S(1)} collective-permute-done((bf16[1024,128]{1,0:T(8,128)(2,1)S(1)}, bf16[1024,128]{1,0:T(8,128)(2,1)S(1)}, u32[]{:S(2)}, u32[]{:S(2)}) %collective-permute-start.2) | collective-permute-done | bytes 262176 | tf_op jit(solution)/shard_map/ppermute | solution.py:14
  106.2 1.5 collective-permute-start.7
  107.7 0.2 multiply_reduce_fusion.2
  107.9 0.0 collective-permute-done
  107.9 0.2 multiply_reduce_fusion.3
  108.1 0.0 collective-permute-done.3
  108.2 0.0 copy-done.1
  108.2 7.9 %fusion.17 = f32[1024,1024]{1,0:T(8,128)} fusion(bf16[1024,1024]{1,0:T(8,128)(2,1)} %collective-permute-done.3, bf16[1024,128]{1,0:T(8,128)(2,1)S(1)} %copy-done.1, bf16[1024,128]{1,0:T(8,128)(2,1)S(1)} %collective-permute-done.2, f32[]{:T(128)} %bitcast.2, f32[1024]{0:T(1024)S(1)} %multiply_reduce_fusion.2, f32[1024]{0:T(1024)S(1)} %multiply_reduce_fusion.5), kind=kOutput, calls=%fused_computation.23 | convolution fusion | flops 2430599168 | bytes 6823940 | tf_op jit(solution)/shard_map/dot_general | solution.py:36
  116.0 0.0 collective-permute-done.1
  116.0 7.8 %fusion.18 = f32[1024,1024]{1,0:T(8,128)} fusion(bf16[1024,1024]{1,0:T(8,128)(2,1)} %collective-permute-done.1, bf16[1024,128]{1,0:T(8,128)(2,1)S(1)} %copy-done.1, bf16[1024,128]{1,0:T(8,128)(2,1)S(1)} %collective-permute-done, f32[]{:T(128)} %bitcast.1, f32[1024]{0:T(1024)S(1)} %multiply_reduce_fusion.3, f32[1024]{0:T(1024)S(1)} %multiply_reduce_fusion.5), kind=kOutput, calls=%fused_computation.24 | convolution fusion | flops 2430599168 | bytes 6823940 | tf_op jit(solution)/shard_map/dot_general | solution.py:36
  123.9 0.0 collective-permute-done.5
  123.9 7.8 %fusion.16 = f32[1024,1024]{1,0:T(8,128)} fusion(bf16[1024,1024]{1,0:T(8,128)(2,1)} %collective-permute-done.5, bf16[1024,128]{1,0:T(8,128)(2,1)S(1)} %copy-done.1, bf16[1024,128]{1,0:T(8,128)(2,1)S(1)} %collective-permute-done.4, f32[]{:T(128)} %bitcast.3, f32[1024]{0:T(1024)S(1)} %multiply_reduce_fusion.1, f32[1024]{0:T(1024)S(1)} %multiply_reduce_fusion.5), kind=kOutput, calls=%fused_computation.22 | convolution fusion | flops 2430599168 | bytes 6823940 | tf_op jit(solution)/shard_map/dot_general | solution.py:36
  131.7 23.2 %collective-permute-done.7 = bf16[1024,1024]{1,0:T(8,128)(2,1)} collective-permute-done((bf16[1024,1024]{1,0:T(8,128)(2,1)}, bf16[1024,1024]{1,0:T(8,128)(2,1)}, u32[]{:S(2)}, u32[]{:S(2)}) %collective-permute-start.7) | collective-permute-done | bytes 2097184 | tf_op jit(solution)/shard_map/ppermute | solution.py:14
  154.9 11.6 %add_convert_fusion = bf16[1024,1024]{1,0:T(8,128)(2,1)} fusion(f32[1024,1024]{1,0:T(8,128)} %fusion.16, f32[1024,1024]{1,0:T(8,128)} %fusion.17, f32[1024,1024]{1,0:T(8,128)} %fusion.19, f32[1024,1024]{1,0:T(8,128)} %fusion.18, bf16[1024,1024]{1,0:T(8,128)(2,1)} %collective-permute-done.7, bf16[1024,128]{1,0:T(8,128)(2,1)S(1)} %copy-done.1, ...), kind=kOutput, calls=%fused_computation.20 | convolution fusion | flops 2435842048 | bytes 21504004 | tf_op jit(solution)/shard_map/dot_general | solution.py:36
  (1 shorter events, 0.0 us)
Async XLA Ops:
  0.0 25.4 %copy-start = (s32[8,5]{1,0:T(8,128)S(1)}, s32[8,5]{1,0:T(8,128)}, u32[]{:S(2)}) copy-start(s32[8,5]{1,0:T(8,128)} %param.7) | copy-start | bytes 484
  0.0 108.1 %collective-permute-start.3 = (bf16[1024,1024]{1,0:T(8,128)(2,1)}, bf16[1024,1024]{1,0:T(8,128)(2,1)}, u32[]{:S(2)}, u32[]{:S(2)}) collective-permute-start(bf16[1024,1024]{1,0:T(8,128)(2,1)} %param.6), channel_id=1, source_target_pairs={{0,4},{4,8},{8,12},{12,16},{16,20},{20,24},{24,28},{1,5},{5,9},{9,... | collective-permute-start | bytes 6291464 | tf_op jit(solution)/shard_map/ppermute | solution.py:14
  12.4 15.8 %collective-permute-start.6 = (bf16[1024,128]{1,0:T(8,128)(2,1)S(1)}, bf16[1024,128]{1,0:T(8,128)(2,1)S(1)}, u32[]{:S(2)}, u32[]{:S(2)}) collective-permute-start(bf16[1024,128]{1,0:T(8,128)(2,1)S(1)} %all_gather.3), channel_id=1, source_target_pairs={{8,0},{12,4},{16,8},{20,12},{24,16},{28,20},{9,1},{13,5},{17,9},{2... | collective-permute-start | bytes 786440 | tf_op jit(solution)/shard_map/ppermute | solution.py:14
  13.6 26.4 %collective-permute-start.4 = (bf16[1024,128]{1,0:T(8,128)(2,1)S(1)}, bf16[1024,128]{1,0:T(8,128)(2,1)S(1)}, u32[]{:S(2)}, u32[]{:S(2)}) collective-permute-start(bf16[1024,128]{1,0:T(8,128)(2,1)S(1)} %all_gather.3), channel_id=1, source_target_pairs={{4,0},{8,4},{12,8},{16,12},{20,16},{24,20},{28,24},{5,1},{9,5},{13... | collective-permute-start | bytes 786440 | tf_op jit(solution)/shard_map/ppermute | solution.py:14
  14.9 91.3 %collective-permute-start.2 = (bf16[1024,128]{1,0:T(8,128)(2,1)S(1)}, bf16[1024,128]{1,0:T(8,128)(2,1)S(1)}, u32[]{:S(2)}, u32[]{:S(2)}) collective-permute-start(bf16[1024,128]{1,0:T(8,128)(2,1)S(1)} %all_gather.3), channel_id=1, source_target_pairs={{0,4},{4,8},{8,12},{12,16},{16,20},{20,24},{24,28},{1,5},{5,9},{9,... | collective-permute-start | bytes 786440 | tf_op jit(solution)/shard_map/ppermute | solution.py:14
  19.5 96.5 %collective-permute-start.1 = (bf16[1024,1024]{1,0:T(8,128)(2,1)}, bf16[1024,1024]{1,0:T(8,128)(2,1)}, u32[]{:S(2)}, u32[]{:S(2)}) collective-permute-start(bf16[1024,1024]{1,0:T(8,128)(2,1)} %param.6), channel_id=1, source_target_pairs={{0,8},{4,12},{8,16},{12,20},{16,24},{20,28},{1,9},{5,13},{9,17},{1... | collective-permute-start | bytes 6291464 | tf_op jit(solution)/shard_map/ppermute | solution.py:14
  28.1 95.7 %collective-permute-start.5 = (bf16[1024,1024]{1,0:T(8,128)(2,1)}, bf16[1024,1024]{1,0:T(8,128)(2,1)}, u32[]{:S(2)}, u32[]{:S(2)}) collective-permute-start(bf16[1024,1024]{1,0:T(8,128)(2,1)} %param.6), channel_id=1, source_target_pairs={{4,0},{8,4},{12,8},{16,12},{20,16},{24,20},{28,24},{5,1},{9,5},{13... | collective-permute-start | bytes 6291464 | tf_op jit(solution)/shard_map/ppermute | solution.py:14
  29.4 78.7 %copy-start.1 = (bf16[1024,128]{1,0:T(8,128)(2,1)S(1)}, bf16[1024,128]{1,0:T(8,128)(2,1)}, u32[]{:S(2)}) copy-start(bf16[1024,128]{1,0:T(8,128)(2,1)} %param.4) | copy-start | bytes 786436
  40.1 67.9 %collective-permute-start = (bf16[1024,128]{1,0:T(8,128)(2,1)S(1)}, bf16[1024,128]{1,0:T(8,128)(2,1)S(1)}, u32[]{:S(2)}, u32[]{:S(2)}) collective-permute-start(bf16[1024,128]{1,0:T(8,128)(2,1)S(1)} %all_gather.3), channel_id=1, source_target_pairs={{0,8},{4,12},{8,16},{12,20},{16,24},{20,28},{1,9},{5,13},{9,17},{1... | collective-permute-start | bytes 786440 | tf_op jit(solution)/shard_map/ppermute | solution.py:14
  106.2 48.7 %collective-permute-start.7 = (bf16[1024,1024]{1,0:T(8,128)(2,1)}, bf16[1024,1024]{1,0:T(8,128)(2,1)}, u32[]{:S(2)}, u32[]{:S(2)}) collective-permute-start(bf16[1024,1024]{1,0:T(8,128)(2,1)} %param.6), channel_id=1, source_target_pairs={{8,0},{12,4},{16,8},{20,12},{24,16},{28,20},{9,1},{13,5},{17,9},{2... | collective-permute-start | bytes 6291464 | tf_op jit(solution)/shard_map/ppermute | solution.py:14
where the time goes:
time: 167 us
  waiting for transfers between devices  62.3 us (37%)
  starting transfers between devices  48.9 us (29%)
  matrix products  43.1 us (26%)
  blocking collectives  5.98 us (4%)
  between operations  3.44 us (2%)
  other arithmetic  2.2 us (1%)
    ppermute x8, waiting for transfers between devices, shifted(): return lax.ppermute(block, axis, route)  62.3 us
    ppermute x8, starting transfers between devices, shifted(): return lax.ppermute(block, axis, route)  48.9 us
    dot_general x5, matrix products, contribute(): return jnp.dot(kern, coef_rows, preferred_element_type=jnp.float32)  43.1 us
    all_gather x1, blocking collectives, per_device(): panel_coords = lax.all_gather(centres, 'ao', axis=0, tiled=True)  5.98 us
  transfers between devices with their start and end apart: 8, of which 2 were waited for; matrix products, arithmetic and copies ran while one was open for 21% of the time, Pallas kernels for 0%

commit v1 on v0

v1 whole, which is shorter than its diff:
```python
import functools
import math

import jax
import jax.numpy as jnp
from jax import lax
from jax.experimental import pallas as pl
from jax.experimental.pallas import tpu as pltpu
from jax.sharding import PartitionSpec as P

RADIUS_FACTOR = 1.3
VMEM_LIMIT = 24 * 1024 * 1024
BF16 = jnp.bfloat16
F32 = jnp.float32
SMEM = pl.BlockSpec(memory_space=pltpu.SMEM)
WHOLE = pl.BlockSpec(memory_space=pltpu.VMEM)


COST = pl.CostEstimate(flops=1 << 20, bytes_accessed=1 << 16, transcendentals=0)


def three_terms(norm):
    high = norm.astype(BF16).astype(F32)
    middle = (norm - high).astype(BF16).astype(F32)
    return high, middle, norm - high - middle


def widened(rows, centre_side):
    wide = rows.astype(F32)
    high, middle, low = three_terms(jnp.sum(wide * wide, axis=1, keepdims=True))
    lane = lax.broadcasted_iota(jnp.int32, (rows.shape[0], 128), 1)
    first, ones = (3, 0) if centre_side else (0, 3)
    extra = jnp.where((lane >= ones) & (lane < ones + 3), 1.0, 0.0)
    extra = jnp.where(lane == first, high, extra)
    extra = jnp.where(lane == first + 1, middle, extra)
    extra = jnp.where(lane == first + 2, low, extra)
    own = (wide * -2.0).astype(BF16) if centre_side else rows
    return jnp.concatenate([own, extra.astype(BF16)], axis=1)


def in_vmem(*arrays):
    return [pltpu.with_memory_space_constraint(array, pltpu.VMEM) for array in arrays]


def kern_kernel(radius, parts, sides, place_ref, pattern_ref, *refs):
    queries, centres = refs[:parts], refs[parts:-3]
    kern_ref, query_wide, centre_wide = refs[-3:]
    me, core, mine = place_ref[0], place_ref[1], place_ref[2]
    side = 1 - 2 * lax.rem(me, 2)
    block_at = lambda steps: me + side * jnp.where(core == 0, steps[0], steps[1])

    rows = query_wide.shape[0] // parts
    for k, piece in enumerate(queries):
        at = pl.multiple_of((mine ^ k) * rows, rows) if parts > 1 else 0
        query_wide[pl.ds(at, rows), :] = widened(piece[...], False)

    depth = centre_wide.shape[0]
    band = pattern_ref.shape[1]
    query_block = jnp.clip(block_at(sides[0]), 0, pattern_ref.shape[0] - 1)
    tile = min(512, query_wide.shape[0])
    columns = min(256, depth)
    for b, (steps, centre) in enumerate(zip(sides[1:], centres)):
        centre_wide[...] = widened(centre[...], True)
        offset = jnp.clip(block_at(steps) - query_block + band // 2, 0, band - 1)
        cut = jnp.where(pattern_ref[query_block, offset] > 0, jnp.float32(radius), jnp.float32(-1.0))

        @pl.loop(0, query_wide.shape[0] // tile)
        def _(row):
            span = pl.ds(pl.multiple_of(row * tile, tile), tile)
            query = query_wide[span, :]
            for start in range(0, depth, columns):
                square = lax.dot_general(
                    query, centre_wide[pl.ds(start, columns), :], (((1,), (1,)), ((), ())), preferred_element_type=F32
                )
                square = jnp.maximum(square, 1e-30)
                dist = square * lax.rsqrt(square)
                inner = jnp.maximum(cut - dist, 0.0)
                inner = inner * inner
                kern_ref[span, pl.ds(b * depth + start, columns)] = (inner * inner * (dist + radius / 4)).astype(BF16)


def kern_blocks(place, pattern, queries, centres, sides):
    parts, blocks = len(queries), len(centres)
    features = queries[0].shape[1]
    query_rows, centre_rows = parts * queries[0].shape[0], centres[0].shape[0]
    return pl.pallas_call(
        functools.partial(kern_kernel, RADIUS_FACTOR * math.sqrt(features), parts, sides),
        in_specs=[SMEM, SMEM] + [WHOLE] * (parts + blocks),
        out_specs=WHOLE,
        out_shape=pltpu.VMEM((query_rows, blocks * centre_rows), BF16),
        scratch_shapes=[
            pltpu.VMEM((query_rows, features + 128), BF16),
            pltpu.VMEM((centre_rows, features + 128), BF16),
        ],
        compiler_params=pltpu.CompilerParams(vmem_limit_bytes=VMEM_LIMIT),
        cost_estimate=COST,
        name="kern",
    )(place, pattern, *queries, *centres)


def score_sum(terms, kern_refs, coef_refs, rows):
    total = None
    for kern, block, coef, column, width in terms:
        depth = coef_refs[coef].shape[0]
        product = jnp.dot(
            kern_refs[kern][rows, pl.ds(block * depth, depth)],
            coef_refs[coef][:, pl.ds(column, width)],
            preferred_element_type=F32,
        )
        total = product if total is None else total + product
    return total


def score_kernel(terms, kerns, tile, *refs):
    out_ref = refs[-1]

    @pl.loop(0, out_ref.shape[0] // tile)
    def _(row):
        rows = pl.ds(pl.multiple_of(row * tile, tile), tile)
        out_ref[rows, :] = score_sum(terms, refs[:kerns], refs[kerns:-1], rows).astype(out_ref.dtype)


def scores(kerns, coefs, terms, dtype):
    rows, width = kerns[0].shape[0], terms[0][4]
    return pl.pallas_call(
        functools.partial(score_kernel, terms, len(kerns), min(256, rows)),
        in_specs=[WHOLE] * (len(kerns) + len(coefs)),
        out_specs=WHOLE,
        out_shape=pltpu.VMEM((rows, width), dtype),
        compiler_params=pltpu.CompilerParams(vmem_limit_bytes=VMEM_LIMIT),
        cost_estimate=COST,
        name="scores",
    )(*in_vmem(*kerns, *coefs))


def final_kernel(terms, scale, tile, column, kern_ref, coef_ref, mid_ref, part_ref, *refs):
    out_ref = refs[-1]
    rows = pl.ds(pl.multiple_of(pl.program_id(0) * tile, tile), tile)
    total = score_sum(terms, [kern_ref], [coef_ref], rows) + part_ref[rows, :].astype(F32)
    total = total + mid_ref[rows, pl.ds(column, total.shape[1])]
    out_ref[...] = (total * scale).astype(out_ref.dtype)


def final(kern, coef, mid, part, scale, half, halves, out):
    rows, width = part.shape
    tile = min(256, rows)
    terms = ((0, 0, 0, 0, width),)
    return pl.pallas_call(
        functools.partial(final_kernel, terms, scale, tile, half * width),
        grid=(rows // tile,),
        in_specs=[WHOLE] * 4 + ([] if out is None else [pl.BlockSpec(memory_space=pl.ANY)]),
        out_specs=pl.BlockSpec((tile, width), lambda r: (r, half)),
        out_shape=jax.ShapeDtypeStruct((rows, width * halves), BF16),
        input_output_aliases={} if out is None else {4: 0},
        compiler_params=pltpu.CompilerParams(vmem_limit_bytes=VMEM_LIMIT),
        cost_estimate=COST,
        name="final",
    )(*in_vmem(kern, coef, mid, part), *([] if out is None else [out]))


def after(array, *others):
    return lax.optimization_barrier((array, *others))[0]


def per_device(queries, centres, coefs, pattern):
    blocks, members = lax.axis_size("pb"), lax.axis_size("ao")
    shares = members // 2
    radius = RADIUS_FACTOR * math.sqrt(queries.shape[1])
    me, member = lax.axis_index("pb"), lax.axis_index("ao")
    core, mine = lax.rem(member, 2), member // 2
    place = jnp.stack([me, core, mine])

    def send(block, *targets):
        route = []
        for i in range(blocks):
            for m in range(members):
                target = targets[m % 2](i)
                if target is not None and 0 <= target[0] < blocks:
                    route.append((i * members + m, target[0] * members + m // 2 * 2 + target[1]))
        return lax.ppermute(block, ("pb", "ao"), route)

    sign = lambda i: 1 - 2 * (i % 2)
    partner = lambda c: lambda i: (i + sign(i), c)
    front = lambda c: lambda i: (i + 2 * sign(i), c)
    back = lambda c: lambda i: (i - 2 * sign(i), c)
    nobody = lambda i: None

    def spread(piece):
        held, step = [piece], 1
        while step < shares:
            route = [(m, m ^ (2 * step)) for m in range(members)]
            held += [lax.ppermute(h, "ao", route) for h in held]
            step *= 2
        return held

    near = send(coefs, partner(0), back(1))
    query_rows = queries.shape[0] // shares
    query_part = lax.dynamic_slice_in_dim(queries, mine * query_rows, query_rows, 0)
    query_t = spread(send(query_part, back(0), partner(1)))
    far_1 = send(coefs, nobody, front(1))
    centre_own = lax.all_gather(centres, "ao", axis=0, tiled=True)
    centre_near = send(centre_own, back(1), partner(0))
    far_source = jnp.where(core == 0, centre_own, centre_near)
    centre_far = send(far_source, front(1), lambda i: (i, 0))

    kern_t = kern_blocks(place, pattern, query_t, [centre_own, centre_near], ((2, 1), (0, 0), (1, 2)))
    pattern_1 = after(pattern, kern_t)
    kern_m = kern_blocks(place, pattern_1, [queries], [centre_own, centre_near], ((0, 0), (0, 0), (1, 2)))
    kern_t = after(kern_t, kern_m)

    width = coefs.shape[1] // 2
    total, part = [], []
    for h in range(2):
        terms = ((0, 0, 0, h * width, width), (0, 1, 1, h * width, width))
        total.append(scores([kern_t], [coefs, near], terms, BF16))
        part.append(send(total[h], front(0), partner(1)))
    coefs_late = after(coefs, total[1])
    far_0 = [send(coefs_late[:, h * width : (h + 1) * width], back(0), nobody) for h in range(2)]
    pattern_2 = after(pattern, total[1])
    kern_far = kern_blocks(place, pattern_2, [queries], [centre_far], ((0, 0), (2, -2)))

    scale = 4.0 / radius**5
    whole = 2 * width
    mid = scores(
        [kern_m, kern_far], [coefs, near, far_1], ((0, 0, 0, 0, whole), (0, 1, 1, 0, whole), (1, 0, 2, 0, whole)), F32
    )
    out = None
    for h in range(2):
        out = final(kern_far, far_0[h], mid, part[h], scale, h, 2, out)
    return out


def solution(mesh):
    in_specs = (P("pb", None), P(("pb", "ao"), None), P("pb", "ao"), P())
    out_specs = P("pb", "ao")
    return jax.shard_map(
        per_device, mesh=mesh, in_specs=in_specs, out_specs=out_specs, check_vma=False
    )
```

time: 167 us -> 83.1 us (0.50)
  waiting for transfers between devices: 62.3 us -> 17.8 us
  matrix products: 43.1 us -> 0 us
  Pallas kernels: 0 us -> 33.1 us
  starting transfers between devices: 48.9 us -> 23.1 us
  between operations: 3.44 us -> 0.23 us
  other arithmetic: 2.2 us -> 0.11 us
    ppermute x8 -> x10, waiting for transfers between devices: 62.3 us -> 17.8 us  [the longest x9 16.4 us: send(): return lax.ppermute(block, ('pb', 'ao'), route)]
    dot_general x5 -> x0, matrix products: 43.1 us -> none  [contribute(): return jnp.dot(kern, coef_rows, preferred_element_type=jnp.float32)]
    pallas_call x0 -> x8, Pallas kernels: none -> 33.1 us  [the longest x3 14.4 us: scores(): pl.pallas_call(functools.partial(score_kernel, terms, len(kerns), min(256...]
    ppermute x8 -> x10, starting transfers between devices: 48.9 us -> 23.1 us  [the longest x9 21.6 us: send(): return lax.ppermute(block, ('pb', 'ao'), route)]
    reduce_sum x6 -> x0, other arithmetic: 2.2 us -> none  [the longest x1 1.16 us: query_norms(): return jnp.sum(query_wide * query_wide, axis=1)[:, None]]
  transfers between devices with their start and end apart: 8 -> 10, of which waited for: 2 -> 4; matrix products, arithmetic and copies ran while one was open for 21% -> 1% of each run, Pallas kernels for 0% -> 37%
where the time goes in v1:
time: 83.1 us; the launch traced here: 82.7 us
  Pallas kernels  33.1 us (40%)
  starting transfers between devices  23.1 us (28%)
  waiting for transfers between devices  17.8 us (21%)
  blocking collectives  6.61 us (8%)
  local copies, waits for them, and re-layouts  1.78 us (2%)
    ppermute x9, starting transfers between devices, send(): return lax.ppermute(block, ('pb', 'ao'), route)  21.6 us
    ppermute x9, waiting for transfers between devices, send(): return lax.ppermute(block, ('pb', 'ao'), route)  16.4 us
    pallas_call x3, Pallas kernels, scores(): pl.pallas_call(functools.partial(score_kernel, terms, len(kerns), min(256...  14.4 us
    pallas_call x3, Pallas kernels, kern_blocks(): pl.pallas_call(functools.partial(kern_kernel, RADIUS_FACTOR * math.sqrt(f...  13.2 us
    all_gather x1, blocking collectives, per_device(): centre_own = lax.all_gather(centres, 'ao', axis=0, tiled=True)  6.61 us
    pallas_call x2, Pallas kernels, final(): pl.pallas_call(functools.partial(final_kernel, terms, scale, tile, half *...  5.54 us
  transfers between devices with their start and end apart: 10, of which 4 were waited for; matrix products, arithmetic and copies ran while one was open for 1% of the time, Pallas kernels for 37%

profile of v1, /device:TPU:0, one launch (start us, length us, event | category | flops | bytes accessed | tf_op | source)
XLA Modules:
  0.0 82.7 jit_solution(6285305136124045886)
XLA Ops:
  0.0 4.8 %collective-permute-start.3 = (bf16[1024,1024]{1,0:T(8,128)(2,1)}, bf16[1024,1024]{1,0:T(8,128)(2,1)S(1)}, u32[]{:S(2)}, u32[]{:S(2)}) collective-permute-start(bf16[1024,1024]{1,0:T(8,128)(2,1)} %refs_1_.3), channel_id=1, source_target_pairs={{0,4},{2,6},{4,0},{5,13},{6,2},{7,15},{8,12},{9,1},{10,14},{11,3},... | collective-permute-start | bytes 6291464 | tf_op jit(solution)/shard_map/ppermute | solution.py:180
  4.8 2.0 %collective-permute-start.6 = (bf16[1024,1024]{1,0:T(8,128)(2,1)}, bf16[1024,1024]{1,0:T(8,128)(2,1)}, u32[]{:S(2)}, u32[]{:S(2)}) collective-permute-start(bf16[1024,1024]{1,0:T(8,128)(2,1)} %refs_1_.3), channel_id=1, source_target_pairs={{1,9},{3,11},{9,17},{11,19},{13,5},{15,7},{17,25},{19,27},{21,13},... | collective-permute-start | bytes 6291464 | tf_op jit(solution)/shard_map/ppermute | solution.py:180
  6.8 6.6 %all_gather.3.refs_2_.refs_1_ = bf16[1024,128]{1,0:T(8,128)(2,1)S(1)} all-gather(bf16[256,128]{1,0:T(8,128)(2,1)} %param.5), channel_id=1, replica_groups=mesh['pb'=8,'ao'=4] {'ao'}, dimensions={0}, use_global_device_ids=true | all-gather | bytes 327680 | tf_op jit(solution)/shard_map/all_gather | solution.py:201
  13.5 1.3 %collective-permute-start.2 = (bf16[1024,128]{1,0:T(8,128)(2,1)S(1)}, bf16[1024,128]{1,0:T(8,128)(2,1)S(1)}, u32[]{:S(2)}, u32[]{:S(2)}) collective-permute-start(bf16[1024,128]{1,0:T(8,128)(2,1)S(1)} %all_gather.3.refs_2_.refs_1_), channel_id=1, source_target_pairs={{1,4},{3,6},{4,13},{5,0},{6,15},{7,2},{8,1},{9,12},{10,3},{11,14},... | collective-permute-start | bytes 786440 | tf_op jit(solution)/shard_map/ppermute | solution.py:180
  14.8 0.9 %constant_dynamic-slice_fusion = bf16[512,128]{1,0:T(8,128)(2,1)S(1)} fusion(bf16[1024,128]{1,0:T(8,128)(2,1)} %refs_0_.3, s32[]{:T(128)S(6)} %select_n.17), kind=kLoop, calls=%fused_computation.2 | loop fusion | bytes 262148 | tf_op jit(solution)/shard_map/dynamic_slice | solution.py:198
  15.7 1.3 %collective-permute-start = (bf16[512,128]{1,0:T(8,128)(2,1)S(1)}, bf16[512,128]{1,0:T(8,128)(2,1)S(1)}, u32[]{:S(2)}, u32[]{:S(2)}) collective-permute-start(bf16[512,128]{1,0:T(8,128)(2,1)S(1)} %constant_dynamic-slice_fusion), channel_id=1, source_target_pairs={{1,5},{3,7},{4,12},{5,1},{6,14},{7,3},{8,0},{9,13},{10,2},{11,15},... | collective-permute-start | bytes 393224 | tf_op jit(solution)/shard_map/ppermute | solution.py:180
  17.0 0.1 pad_add_fusion.place_ref
  17.1 10.3 %collective-permute-done.refs_0_ = bf16[512,128]{1,0:T(8,128)(2,1)S(1)} collective-permute-done((bf16[512,128]{1,0:T(8,128)(2,1)S(1)}, bf16[512,128]{1,0:T(8,128)(2,1)S(1)}, u32[]{:S(2)}, u32[]{:S(2)}) %collective-permute-start) | collective-permute-done | bytes 131104 | tf_op jit(solution)/shard_map/ppermute | solution.py:180
  27.3 1.5 %collective-permute-start.1 = (bf16[512,128]{1,0:T(8,128)(2,1)S(1)}, bf16[512,128]{1,0:T(8,128)(2,1)S(1)}, u32[]{:S(2)}, u32[]{:S(2)}) collective-permute-start(bf16[512,128]{1,0:T(8,128)(2,1)S(1)} %collective-permute-done.refs_0_), channel_id=1, source_target_pairs={{0,2},{1,3},{2,0},{3,1},{4,6},{5,7},{6,4},{7,5},{8,10},{9,11},{10,... | collective-permute-start | bytes 393224 | tf_op jit(solution)/shard_map/ppermute | solution.py:192
  28.8 0.0 collective-permute-done.2.refs_3_.refs_2_
  28.9 0.0 copy-start.1
  28.9 2.1 %collective-permute-start.4 = (bf16[1024,128]{1,0:T(8,128)(2,1)S(1)}, bf16[1024,128]{1,0:T(8,128)(2,1)S(1)}, u32[]{:S(2)}, u32[]{:S(2)}) collective-permute-start(bf16[1024,128]{1,0:T(8,128)(2,1)S(1)} %broadcast_select_fusion), channel_id=1, source_target_pairs={{0,9},{1,0},{2,11},{3,2},{5,4},{7,6},{8,17},{9,8},{10,19},{11,10},... | collective-permute-start | bytes 786440 | tf_op jit(solution)/shard_map/ppermute | solution.py:180
  31.0 1.4 %collective-permute-done.1.refs_1_ = bf16[512,128]{1,0:T(8,128)(2,1)S(1)} collective-permute-done((bf16[512,128]{1,0:T(8,128)(2,1)S(1)}, bf16[512,128]{1,0:T(8,128)(2,1)S(1)}, u32[]{:S(2)}, u32[]{:S(2)}) %collective-permute-start.1) | collective-permute-done | bytes 131104 | tf_op jit(solution)/shard_map/ppermute | solution.py:192
  32.3 0.0 copy-start.2
  32.3 0.7 copy-done.2
  33.0 5.1 %kern.3.refs_0_ = bf16[1024,2048]{1,0:T(8,128)(2,1)S(1)} custom-call(s32[3]{0:T(128)S(1)} %pad_add_fusion.place_ref, s32[8,5]{1,0:T(8,128)S(1)} %copy-done.2, bf16[512,128]{1,0:T(8,128)(2,1)S(1)} %collective-permute-done.refs_0_, bf16[512,128]{1,0:T(8,128)(2,1)S(1)} %collective-permute-done.1.refs_1_, bf16[1024,128]{1,0:T(8,128)(2,1)S(1)} %all_gather.3.refs_2_.refs_1_, ...), custom_call_target="tpu_custom_call" | custom-call | flops 1048576 | bytes 65536 | tf_op jit(solution)/shard_map/kern/pallas_call | solution.py:86
  38.1 0.0 copy-done.1
  38.1 0.0 copy-start
  38.2 5.1 %kern.4.refs_0_ = bf16[1024,2048]{1,0:T(8,128)(2,1)S(1)} custom-call(s32[3]{0:T(128)S(1)} %pad_add_fusion.place_ref, s32[8,5]{1,0:T(8,128)S(1)} %copy-done.2, bf16[1024,128]{1,0:T(8,128)(2,1)S(1)} %copy-done.1, bf16[1024,128]{1,0:T(8,128)(2,1)S(1)} %all_gather.3.refs_2_.refs_1_, bf16[1024,128]{1,0:T(8,128)(2,1)S(1)} %collective-permute-done.2.refs_3_.refs_2_), custom_call_target="tpu_custom_call" | custom-call | flops 1048576 | bytes 65536 | tf_op jit(solution)/shard_map/kern/pallas_call | solution.py:86
  43.3 0.0 collective-permute-done.3.refs_2_.refs_3_
  43.3 0.0 copy-done
  43.3 2.8 %scores.3 = bf16[1024,512]{1,0:T(8,128)(2,1)S(1)} custom-call(bf16[1024,2048]{1,0:T(8,128)(2,1)S(1)} %kern.3.refs_0_, bf16[1024,1024]{1,0:T(8,128)(2,1)S(1)} %copy-done, bf16[1024,1024]{1,0:T(8,128)(2,1)S(1)} %collective-permute-done.3.refs_2_.refs_3_), custom_call_target="tpu_custom_call" | custom-call | flops 1048576 | bytes 65536 | tf_op jit(solution)/shard_map/scores/pallas_call | solution.py:125
  46.1 2.8 %scores.5 = bf16[1024,512]{1,0:T(8,128)(2,1)S(1)} custom-call(bf16[1024,2048]{1,0:T(8,128)(2,1)S(1)} %kern.3.refs_0_, bf16[1024,1024]{1,0:T(8,128)(2,1)S(1)} %copy-done, bf16[1024,1024]{1,0:T(8,128)(2,1)S(1)} %collective-permute-done.3.refs_2_.refs_3_), custom_call_target="tpu_custom_call" | custom-call | flops 1048576 | bytes 65536 | tf_op jit(solution)/shard_map/scores/pallas_call | solution.py:125
  49.0 2.9 %collective-permute-start.9 = (bf16[1024,512]{1,0:T(8,128)(2,1)S(1)}, bf16[1024,512]{1,0:T(8,128)(2,1)S(1)}, u32[]{:S(2)}, u32[]{:S(2)}) collective-permute-start(bf16[1024,512]{1,0:T(8,128)(2,1)S(1)} %scores.5), channel_id=1, source_target_pairs={{0,8},{1,5},{2,10},{3,7},{5,1},{7,3},{8,16},{9,13},{10,18},{11,15}... | collective-permute-start | bytes 3145736 | tf_op jit(solution)/shard_map/ppermute | solution.py:180
  51.9 0.2 fusion
  52.1 1.3 %collective-permute-start.8 = (bf16[1024,512]{1,0:T(8,128)(2,1)S(1)}, bf16[1024,512]{1,0:T(8,128)(2,1)S(1)}, u32[]{:S(2)}, u32[]{:S(2)}) collective-permute-start(bf16[1024,512]{1,0:T(8,128)(2,1)S(1)} %get-tuple-element.13), channel_id=1, source_target_pairs={{4,12},{6,14},{8,0},{10,2},{12,20},{14,22},{16,8},{18,10},{20,28},... | collective-permute-start | bytes 3145736 | tf_op jit(solution)/shard_map/ppermute | solution.py:180
  53.4 4.6 %collective-permute-start.7 = (bf16[1024,512]{1,0:T(8,128)(2,1)S(1)}, bf16[1024,512]{1,0:T(8,128)(2,1)S(1)}, u32[]{:S(2)}, u32[]{:S(2)}) collective-permute-start(bf16[1024,512]{1,0:T(8,128)(2,1)S(1)} %scores.3), channel_id=1, source_target_pairs={{0,8},{1,5},{2,10},{3,7},{5,1},{7,3},{8,16},{9,13},{10,18},{11,15}... | collective-permute-start | bytes 3145736 | tf_op jit(solution)/shard_map/ppermute | solution.py:180
  58.0 0.0 collective-permute-done.4.refs_1_
  58.0 1.3 %collective-permute-start.5 = (bf16[1024,512]{1,0:T(8,128)(2,1)S(1)}, bf16[1024,512]{1,0:T(8,128)(2,1)S(1)}, u32[]{:S(2)}, u32[]{:S(2)}) collective-permute-start(bf16[1024,512]{1,0:T(8,128)(2,1)S(1)} %get-tuple-element.14), channel_id=1, source_target_pairs={{4,12},{6,14},{8,0},{10,2},{12,20},{14,22},{16,8},{18,10},{20,28},... | collective-permute-start | bytes 3145736 | tf_op jit(solution)/shard_map/ppermute | solution.py:180
  59.3 3.0 %kern.5.refs_1_.kern_ref = bf16[1024,1024]{1,0:T(8,128)(2,1)S(1)} custom-call(s32[3]{0:T(128)S(1)} %pad_add_fusion.place_ref, s32[8,5]{1,0:T(8,128)S(1)} %copy-done.2, bf16[1024,128]{1,0:T(8,128)(2,1)S(1)} %copy-done.1, bf16[1024,128]{1,0:T(8,128)(2,1)S(1)} %collective-permute-done.4.refs_1_), custom_call_target="tpu_custom_call" | custom-call | flops 1048576 | bytes 65536 | tf_op jit(solution)/shard_map/kern/pallas_call | solution.py:86
  62.3 0.0 collective-permute-done.6.refs_4_
  62.3 8.8 %scores.4.mid_ref = f32[1024,1024]{1,0:T(8,128)S(1)} custom-call(bf16[1024,2048]{1,0:T(8,128)(2,1)S(1)} %kern.4.refs_0_, bf16[1024,1024]{1,0:T(8,128)(2,1)S(1)} %kern.5.refs_1_.kern_ref, bf16[1024,1024]{1,0:T(8,128)(2,1)S(1)} %copy-done, bf16[1024,1024]{1,0:T(8,128)(2,1)S(1)} %collective-permute-done.3.refs_2_.refs_3_, ...), custom_call_target="tpu_custom_call" | custom-call | flops 1048576 | bytes 65536 | tf_op jit(solution)/shard_map/scores/pallas_call | solution.py:125
  71.0 0.0 collective-permute-done.9.part_ref
  71.0 0.0 collective-permute-done.8.coef_ref
  71.0 2.8 %final.2.refs_0_ = bf16[1024,1024]{1,0:T(8,128)(2,1)} custom-call(bf16[1024,1024]{1,0:T(8,128)(2,1)S(1)} %kern.5.refs_1_.kern_ref, bf16[1024,512]{1,0:T(8,128)(2,1)S(1)} %collective-permute-done.8.coef_ref, f32[1024,1024]{1,0:T(8,128)S(1)} %scores.4.mid_ref, bf16[1024,512]{1,0:T(8,128)(2,1)S(1)} %collective-permute-done.9.part_ref), custom_call_target="tpu_custom_call" | custom-call | flops 1048576 | bytes 65536 | tf_op jit(solution)/shard_map/final/pallas_call | solution.py:148
  73.8 1.5 %collective-permute-done.7.part_ref = bf16[1024,512]{1,0:T(8,128)(2,1)S(1)} collective-permute-done((bf16[1024,512]{1,0:T(8,128)(2,1)S(1)}, bf16[1024,512]{1,0:T(8,128)(2,1)S(1)}, u32[]{:S(2)}, u32[]{:S(2)}) %collective-permute-start.7) | collective-permute-done | bytes 1048608 | tf_op jit(solution)/shard_map/ppermute | solution.py:180
  75.4 4.6 %collective-permute-done.5.coef_ref = bf16[1024,512]{1,0:T(8,128)(2,1)S(1)} collective-permute-done((bf16[1024,512]{1,0:T(8,128)(2,1)S(1)}, bf16[1024,512]{1,0:T(8,128)(2,1)S(1)}, u32[]{:S(2)}, u32[]{:S(2)}) %collective-permute-start.5) | collective-permute-done | bytes 1048608 | tf_op jit(solution)/shard_map/ppermute | solution.py:180
  80.0 2.8 %final.3 = bf16[1024,1024]{1,0:T(8,128)(2,1)} custom-call(bf16[1024,1024]{1,0:T(8,128)(2,1)S(1)} %kern.5.refs_1_.kern_ref, bf16[1024,512]{1,0:T(8,128)(2,1)S(1)} %collective-permute-done.5.coef_ref, f32[1024,1024]{1,0:T(8,128)S(1)} %scores.4.mid_ref, bf16[1024,512]{1,0:T(8,128)(2,1)S(1)} %collective-permute-done.7.part_ref, ...), custom_call_target="tpu_custom_call", output_to_operand_aliasing={{}: (4, {})} | custom-call | flops 1048576 | bytes 65536 | tf_op jit(solution)/shard_map/final/pallas_call | solution.py:148
  (1 shorter events, 0.0 us)
Async XLA Ops:
  0.0 43.3 %collective-permute-start.3 = (bf16[1024,1024]{1,0:T(8,128)(2,1)}, bf16[1024,1024]{1,0:T(8,128)(2,1)S(1)}, u32[]{:S(2)}, u32[]{:S(2)}) collective-permute-start(bf16[1024,1024]{1,0:T(8,128)(2,1)} %refs_1_.3), channel_id=1, source_target_pairs={{0,4},{2,6},{4,0},{5,13},{6,2},{7,15},{8,12},{9,1},{10,14},{11,3},... | collective-permute-start | bytes 6291464 | tf_op jit(solution)/shard_map/ppermute | solution.py:180
  4.8 57.4 %collective-permute-start.6 = (bf16[1024,1024]{1,0:T(8,128)(2,1)}, bf16[1024,1024]{1,0:T(8,128)(2,1)}, u32[]{:S(2)}, u32[]{:S(2)}) collective-permute-start(bf16[1024,1024]{1,0:T(8,128)(2,1)} %refs_1_.3), channel_id=1, source_target_pairs={{1,9},{3,11},{9,17},{11,19},{13,5},{15,7},{17,25},{19,27},{21,13},... | collective-permute-start | bytes 6291464 | tf_op jit(solution)/shard_map/ppermute | solution.py:180
  13.5 15.4 %collective-permute-start.2 = (bf16[1024,128]{1,0:T(8,128)(2,1)S(1)}, bf16[1024,128]{1,0:T(8,128)(2,1)S(1)}, u32[]{:S(2)}, u32[]{:S(2)}) collective-permute-start(bf16[1024,128]{1,0:T(8,128)(2,1)S(1)} %all_gather.3.refs_2_.refs_1_), channel_id=1, source_target_pairs={{1,4},{3,6},{4,13},{5,0},{6,15},{7,2},{8,1},{9,12},{10,3},{11,14},... | collective-permute-start | bytes 786440 | tf_op jit(solution)/shard_map/ppermute | solution.py:180
  15.7 11.7 %collective-permute-start = (bf16[512,128]{1,0:T(8,128)(2,1)S(1)}, bf16[512,128]{1,0:T(8,128)(2,1)S(1)}, u32[]{:S(2)}, u32[]{:S(2)}) collective-permute-start(bf16[512,128]{1,0:T(8,128)(2,1)S(1)} %constant_dynamic-slice_fusion), channel_id=1, source_target_pairs={{1,5},{3,7},{4,12},{5,1},{6,14},{7,3},{8,0},{9,13},{10,2},{11,15},... | collective-permute-start | bytes 393224 | tf_op jit(solution)/shard_map/ppermute | solution.py:180
  27.3 5.0 %collective-permute-start.1 = (bf16[512,128]{1,0:T(8,128)(2,1)S(1)}, bf16[512,128]{1,0:T(8,128)(2,1)S(1)}, u32[]{:S(2)}, u32[]{:S(2)}) collective-permute-start(bf16[512,128]{1,0:T(8,128)(2,1)S(1)} %collective-permute-done.refs_0_), channel_id=1, source_target_pairs={{0,2},{1,3},{2,0},{3,1},{4,6},{5,7},{6,4},{7,5},{8,10},{9,11},{10,... | collective-permute-start | bytes 393224 | tf_op jit(solution)/shard_map/ppermute | solution.py:192
  28.9 9.3 %copy-start.1 = (bf16[1024,128]{1,0:T(8,128)(2,1)S(1)}, bf16[1024,128]{1,0:T(8,128)(2,1)}, u32[]{:S(2)}) copy-start(bf16[1024,128]{1,0:T(8,128)(2,1)} %refs_0_.3) | copy-start | bytes 786436
  28.9 29.1 %collective-permute-start.4 = (bf16[1024,128]{1,0:T(8,128)(2,1)S(1)}, bf16[1024,128]{1,0:T(8,128)(2,1)S(1)}, u32[]{:S(2)}, u32[]{:S(2)}) collective-permute-start(bf16[1024,128]{1,0:T(8,128)(2,1)S(1)} %broadcast_select_fusion), channel_id=1, source_target_pairs={{0,9},{1,0},{2,11},{3,2},{5,4},{7,6},{8,17},{9,8},{10,19},{11,10},... | collective-permute-start | bytes 786440 | tf_op jit(solution)/shard_map/ppermute | solution.py:180
  32.3 0.7 copy-start.2
  38.1 5.1 %copy-start = (bf16[1024,1024]{1,0:T(8,128)(2,1)S(1)}, bf16[1024,1024]{1,0:T(8,128)(2,1)}, u32[]{:S(2)}) copy-start(bf16[1024,1024]{1,0:T(8,128)(2,1)} %refs_1_.3) | copy-start | bytes 6291460
  49.0 22.1 %collective-permute-start.9 = (bf16[1024,512]{1,0:T(8,128)(2,1)S(1)}, bf16[1024,512]{1,0:T(8,128)(2,1)S(1)}, u32[]{:S(2)}, u32[]{:S(2)}) collective-permute-start(bf16[1024,512]{1,0:T(8,128)(2,1)S(1)} %scores.5), channel_id=1, source_target_pairs={{0,8},{1,5},{2,10},{3,7},{5,1},{7,3},{8,16},{9,13},{10,18},{11,15}... | collective-permute-start | bytes 3145736 | tf_op jit(solution)/shard_map/ppermute | solution.py:180
  52.1 19.0 %collective-permute-start.8 = (bf16[1024,512]{1,0:T(8,128)(2,1)S(1)}, bf16[1024,512]{1,0:T(8,128)(2,1)S(1)}, u32[]{:S(2)}, u32[]{:S(2)}) collective-permute-start(bf16[1024,512]{1,0:T(8,128)(2,1)S(1)} %get-tuple-element.13), channel_id=1, source_target_pairs={{4,12},{6,14},{8,0},{10,2},{12,20},{14,22},{16,8},{18,10},{20,28},... | collective-permute-start | bytes 3145736 | tf_op jit(solution)/shard_map/ppermute | solution.py:180
  53.4 22.0 %collective-permute-start.7 = (bf16[1024,512]{1,0:T(8,128)(2,1)S(1)}, bf16[1024,512]{1,0:T(8,128)(2,1)S(1)}, u32[]{:S(2)}, u32[]{:S(2)}) collective-permute-start(bf16[1024,512]{1,0:T(8,128)(2,1)S(1)} %scores.3), channel_id=1, source_target_pairs={{0,8},{1,5},{2,10},{3,7},{5,1},{7,3},{8,16},{9,13},{10,18},{11,15}... | collective-permute-start | bytes 3145736 | tf_op jit(solution)/shard_map/ppermute | solution.py:180
  58.0 22.0 %collective-permute-start.5 = (bf16[1024,512]{1,0:T(8,128)(2,1)S(1)}, bf16[1024,512]{1,0:T(8,128)(2,1)S(1)}, u32[]{:S(2)}, u32[]{:S(2)}) collective-permute-start(bf16[1024,512]{1,0:T(8,128)(2,1)S(1)} %get-tuple-element.14), channel_id=1, source_target_pairs={{4,12},{6,14},{8,0},{10,2},{12,20},{14,22},{16,8},{18,10},{20,28},... | collective-permute-start | bytes 3145736 | tf_op jit(solution)/shard_map/ppermute | solution.py:180

commit v2 on v1

v2 whole, which is shorter than its diff:
```python
import functools
import math

import jax
import jax.numpy as jnp
from jax import lax
from jax.experimental import pallas as pl
from jax.experimental.pallas import tpu as pltpu
from jax.sharding import PartitionSpec as P

RADIUS_FACTOR = 1.3
VMEM_LIMIT = 24 * 1024 * 1024
BF16 = jnp.bfloat16
F32 = jnp.float32
SMEM = pl.BlockSpec(memory_space=pltpu.SMEM)
WHOLE = pl.BlockSpec(memory_space=pltpu.VMEM)


COST = pl.CostEstimate(flops=1 << 20, bytes_accessed=1 << 16, transcendentals=0)


def three_terms(norm):
    high = norm.astype(BF16).astype(F32)
    middle = (norm - high).astype(BF16).astype(F32)
    return high, middle, norm - high - middle


def widened(rows, centre_side):
    wide = rows.astype(F32)
    high, middle, low = three_terms(jnp.sum(wide * wide, axis=1, keepdims=True))
    lane = lax.broadcasted_iota(jnp.int32, (rows.shape[0], 128), 1)
    first, ones = (3, 0) if centre_side else (0, 3)
    extra = jnp.where((lane >= ones) & (lane < ones + 3), 1.0, 0.0)
    extra = jnp.where(lane == first, high, extra)
    extra = jnp.where(lane == first + 1, middle, extra)
    extra = jnp.where(lane == first + 2, low, extra)
    own = (wide * -2.0).astype(BF16) if centre_side else rows
    return jnp.concatenate([own, extra.astype(BF16)], axis=1)


def in_vmem(*arrays):
    return [pltpu.with_memory_space_constraint(array, pltpu.VMEM) for array in arrays]


def kern_tile(query, centre_wide, cut, radius, put):
    depth = centre_wide.shape[0]
    columns = min(256, depth)
    for start in range(0, depth, columns):
        span = pl.ds(start, columns)
        square = lax.dot_general(
            query, centre_wide[span, :], (((1,), (1,)), ((), ())), preferred_element_type=F32
        )
        square = jnp.maximum(square, 1e-30)
        dist = square * lax.rsqrt(square)
        inner = jnp.maximum(cut - dist, 0.0)
        inner = inner * inner
        put(span, (inner * inner * (dist + radius / 4)).astype(BF16))


def kern_kernel(radius, steps, sources, scored, carried, halves, place_ref, pattern_ref, query_ref, *refs):
    centre = refs[0][...]
    for source in refs[1:sources]:
        centre = centre + source[...]
    extra = refs[sources : sources + scored]
    first = sources + scored + carried
    out_ref, *half_refs = refs[first : first + 1 + halves]
    query_wide, centre_wide, *scratch = refs[first + 1 + halves :]
    copies = []
    if scored:
        kern_ref, coef_ref, sems = scratch
        copies.append(pltpu.make_async_copy(extra[0], coef_ref, sems.at[0]))
        for h, half_ref in enumerate(half_refs):
            columns = pl.ds(h * half_ref.shape[1], half_ref.shape[1])
            copies.append(pltpu.make_async_copy(refs[first - 1].at[:, columns], half_ref, sems.at[1 + h]))
    for copy in copies:
        copy.start()

    query_wide[...] = widened(query_ref[...], False)
    centre_wide[...] = widened(centre, True)
    me, core = place_ref[0], place_ref[1]
    side = 1 - 2 * lax.rem(me, 2)
    blocks, band = pattern_ref.shape
    query_block, centre_block = (me + side * jnp.where(core == 0, step[0], step[1]) for step in steps)
    query_block = jnp.clip(query_block, 0, blocks - 1)
    offset = jnp.clip(centre_block - query_block + band // 2, 0, band - 1)
    cut = jnp.where(pattern_ref[query_block, offset] > 0, jnp.float32(radius), jnp.float32(-1.0))

    tile = min(512, query_wide.shape[0])
    for row in range(query_wide.shape[0] // tile):
        rows = pl.ds(row * tile, tile)

        def put(span, value):
            if scored:
                kern_ref[:, span] = value
            else:
                out_ref[rows, span] = value

        kern_tile(query_wide[rows, :], centre_wide, cut, radius, put)
        if row == 0:
            for copy in copies:
                copy.wait()
        if scored:
            total = jnp.dot(kern_ref[...], coef_ref[...], preferred_element_type=F32)
            total = total + extra[1][rows, :].astype(F32) if scored == 2 else total
            out_ref[rows, :] = total.astype(out_ref.dtype)


def kern_blocks(place, pattern, queries, centres, steps, coefs=None, add=None, dtype=BF16, halves=0, carry=None):
    query_rows, features = queries.shape
    centre_rows = centres[0].shape[0]
    scratch = [
        pltpu.VMEM((query_rows, features + 128), BF16),
        pltpu.VMEM((centre_rows, features + 128), BF16),
    ]
    extra, specs, out_shape = [], [], pltpu.VMEM((query_rows, centre_rows), BF16)
    if coefs is not None:
        width = coefs.shape[1]
        extra, specs, out_shape = [coefs], [pl.BlockSpec(memory_space=pl.ANY)], pltpu.VMEM((query_rows, width), dtype)
        scratch += [
            pltpu.VMEM((min(512, query_rows), centre_rows), BF16),
            pltpu.VMEM(coefs.shape, BF16),
            pltpu.SemaphoreType.DMA((1 + halves,)),
        ]
        if halves:
            out_shape = [out_shape] + [pltpu.VMEM((centre_rows, carry.shape[1] // halves), BF16)] * halves
    if add is not None:
        extra, specs = extra + in_vmem(add), specs + [WHOLE]
    scored = len(extra)
    if carry is not None:
        extra, specs = extra + [carry], specs + [pl.BlockSpec(memory_space=pl.ANY)]
    return pl.pallas_call(
        functools.partial(
            kern_kernel, RADIUS_FACTOR * math.sqrt(features), steps, len(centres), scored, len(extra) - scored, halves
        ),
        in_specs=[SMEM, SMEM] + [WHOLE] * (1 + len(centres)) + specs,
        out_specs=[WHOLE] * (1 + halves) if halves else WHOLE,
        out_shape=out_shape,
        scratch_shapes=scratch,
        compiler_params=pltpu.CompilerParams(vmem_limit_bytes=VMEM_LIMIT),
        cost_estimate=COST,
        name="kern",
    )(place, pattern, queries, *centres, *extra)


def score_sum(terms, kern_refs, coef_refs, rows):
    total = None
    for kern, block, coef, column, width in terms:
        depth = coef_refs[coef].shape[0]
        product = jnp.dot(
            kern_refs[kern][rows, pl.ds(block * depth, depth)],
            coef_refs[coef][:, pl.ds(column, width)],
            preferred_element_type=F32,
        )
        total = product if total is None else total + product
    return total


def score_kernel(terms, kerns, adds, column, tile, *refs):
    out_ref = refs[-1]
    coefs = refs[kerns : len(refs) - 1 - adds]

    @pl.loop(0, out_ref.shape[0] // tile)
    def _(row):
        rows = pl.ds(pl.multiple_of(row * tile, tile), tile)
        total = score_sum(terms, refs[:kerns], coefs, rows)
        if adds:
            total = total + refs[-2][rows, pl.ds(column, total.shape[1])].astype(F32)
        out_ref[rows, :] = total.astype(out_ref.dtype)


def scores(kerns, coefs, terms, dtype, add=None, column=0):
    rows, width = kerns[0].shape[0], terms[0][4]
    adds = [] if add is None else [add]
    return pl.pallas_call(
        functools.partial(score_kernel, terms, len(kerns), len(adds), column, min(256, rows)),
        in_specs=[WHOLE] * (len(kerns) + len(coefs) + len(adds)),
        out_specs=WHOLE,
        out_shape=pltpu.VMEM((rows, width), dtype),
        compiler_params=pltpu.CompilerParams(vmem_limit_bytes=VMEM_LIMIT),
        cost_estimate=COST,
        name="scores",
    )(*in_vmem(*kerns, *coefs, *adds))


def final_kernel(scale, tile, column, place_ref, kern_ref, far_0_ref, far_1_ref, mid_ref, part_ref, *refs):
    out_ref = refs[-1]
    core = place_ref[1]
    rows = pl.ds(pl.multiple_of(pl.program_id(0) * tile, tile), tile)
    columns = pl.ds(column, out_ref.shape[1])

    def finish(coefs):
        total = jnp.dot(kern_ref[rows, :], coefs, preferred_element_type=F32)
        total = total + part_ref[rows, :].astype(F32) + mid_ref[rows, columns]
        out_ref[...] = (total * scale).astype(out_ref.dtype)

    @pl.when(core == 0)
    def _():
        finish(far_0_ref[...])

    @pl.when(core == 1)
    def _():
        finish(far_1_ref[:, columns])


def final(place, kern, far_0, far_1, mid, part, scale, half, halves, out):
    rows, width = part.shape
    tile = min(512, rows)
    return pl.pallas_call(
        functools.partial(final_kernel, scale, tile, half * width),
        grid=(rows // tile,),
        in_specs=[SMEM] + [WHOLE] * 5 + ([] if out is None else [pl.BlockSpec(memory_space=pl.ANY)]),
        out_specs=pl.BlockSpec((tile, width), lambda r: (r, half)),
        out_shape=jax.ShapeDtypeStruct((rows, width * halves), BF16),
        input_output_aliases={} if out is None else {6: 0},
        compiler_params=pltpu.CompilerParams(vmem_limit_bytes=VMEM_LIMIT),
        cost_estimate=COST,
        name="final",
    )(place, *in_vmem(kern, far_0, far_1, mid, part), *([] if out is None else [out]))


def after(array, *others):
    return lax.optimization_barrier((array, *others))[0]


def per_device(queries, centres, coefs, pattern):
    blocks, members = lax.axis_size("pb"), lax.axis_size("ao")
    radius = RADIUS_FACTOR * math.sqrt(queries.shape[1])
    me, core = lax.axis_index("pb"), lax.rem(lax.axis_index("ao"), 2)
    place = jnp.stack([me, core])

    def send(block, *targets):
        route = []
        for i in range(blocks):
            for m in range(members):
                target = targets[m % 2](i)
                if target is not None and 0 <= target[0] < blocks:
                    route.append((i * members + m, target[0] * members + m // 2 * 2 + target[1]))
        return lax.ppermute(block, ("pb", "ao"), route)

    sign = lambda i: 1 - 2 * (i % 2)
    partner = lambda c: lambda i: (i + sign(i), c)
    front = lambda c: lambda i: (i + 2 * sign(i), c)
    back = lambda c: lambda i: (i - 2 * sign(i), c)
    nobody = lambda i: None

    near = send(coefs, partner(0), back(1))
    query_t = send(queries, back(0), partner(1))
    far_1 = send(coefs, nobody, front(1))
    centre_own = lax.all_gather(centres, "ao", axis=0, tiled=True)
    centre_near = send(after(centre_own, query_t), back(1), partner(0))

    def kern(order, query_block, centre_block, query_at, centre_at, *scored):
        return kern_blocks(after(place, *order), pattern, query_block, centre_block, (query_at, centre_at), *scored)

    at_me, at_target, at_near, at_far = (0, 0), (2, 1), (1, 2), (2, -2)
    width = coefs.shape[1] // 2
    coefs_hbm = pltpu.with_memory_space_constraint(coefs, pltpu.HBM)
    base_t = kern((), query_t, [centre_own], at_target, at_me, coefs_hbm)
    base_m, *halves = kern((base_t,), queries, [centre_own], at_me, at_me, coefs_hbm, None, BF16, 2, coefs_hbm)
    kern_t = kern((base_m,), query_t, [centre_near], at_target, at_near)

    total, part = [], []
    for h in range(2):
        total.append(scores([kern_t], [near], ((0, 0, 0, h * width, width),), BF16, base_t, h * width))
        part.append(send(total[h], front(0), partner(1)))
    far_0 = [send(after(halves[0], kern_t), back(0), nobody), send(after(halves[1], total[0], far_1), back(0), nobody)]
    centre_far_0 = send(after(centre_near, total[1]), nobody, lambda i: (i, 0))
    centre_far_1 = send(after(centre_own, total[1]), nobody, front(1))
    mid, far_1 = kern((total[1],), queries, [centre_near], at_me, at_near, near, base_m, F32, 1, far_1)
    kern_far = kern((mid,), queries, [centre_far_0, centre_far_1], at_me, at_far)

    scale = 4.0 / radius**5
    out = None
    for h in range(2):
        out = final(place, kern_far, far_0[h], far_1, mid, part[h], scale, h, 2, out)
    return out


def solution(mesh):
    in_specs = (P("pb", None), P(("pb", "ao"), None), P("pb", "ao"), P())
    out_specs = P("pb", "ao")
    return jax.shard_map(
        per_device, mesh=mesh, in_specs=in_specs, out_specs=out_specs, check_vma=False
    )
```

time: 83.1 us -> 73.6 us (0.89)
  the two profiles are of different devices: /device:TPU:0 before, /device:TPU:10 now
where the time goes in v2:
time: 73.6 us; the launch traced here: 73.2 us
  Pallas kernels  30.7 us (42%)
  starting transfers between devices  25.6 us (35%)
  waiting for transfers between devices  9.97 us (14%)
  blocking collectives  6 us (8%)
    ppermute x10, starting transfers between devices, send(): return lax.ppermute(block, ('pb', 'ao'), route)  25.6 us
    pallas_call x5, Pallas kernels, kern_blocks(): pl.pallas_call(functools.partial(kern_kernel, RADIUS_FACTOR * math.sqrt(f...  21.4 us
    ppermute x10, waiting for transfers between devices, send(): return lax.ppermute(block, ('pb', 'ao'), route)  9.97 us
    all_gather x1, blocking collectives, per_device(): centre_own = lax.all_gather(centres, 'ao', axis=0, tiled=True)  6 us
    pallas_call x2, Pallas kernels, final(): pl.pallas_call(functools.partial(final_kernel, scale, tile, half * width)...  5.75 us
    pallas_call x2, Pallas kernels, scores(): pl.pallas_call(functools.partial(score_kernel, terms, len(kerns), len(add...  3.51 us
  transfers between devices with their start and end apart: 10, of which 3 were waited for; matrix products, arithmetic and copies ran while one was open for 0% of the time, Pallas kernels for 38%

profile of v2, /device:TPU:10, one launch (start us, length us, event | category | flops | bytes accessed | tf_op | source)
XLA Modules:
  0.0 73.2 jit_solution(17105371002909698815)
XLA Ops:
  0.0 2.4 %collective-permute-start.2 = (bf16[1024,1024]{1,0:T(8,128)(2,1)}, bf16[1024,1024]{1,0:T(8,128)(2,1)S(1)}, u32[]{:S(2)}, u32[]{:S(2)}) collective-permute-start(bf16[1024,1024]{1,0:T(8,128)(2,1)} %refs_2_.1), channel_id=1, source_target_pairs={{0,4},{2,6},{4,0},{5,13},{6,2},{7,15},{8,12},{9,1},{10,14},{11,3},... | collective-permute-start | bytes 6291464 | tf_op jit(solution)/shard_map/ppermute | solution.py:238
  2.4 2.0 %collective-permute-start.3 = (bf16[1024,1024]{1,0:T(8,128)(2,1)}, bf16[1024,1024]{1,0:T(8,128)(2,1)}, u32[]{:S(2)}, u32[]{:S(2)}) collective-permute-start(bf16[1024,1024]{1,0:T(8,128)(2,1)} %refs_2_.1), channel_id=1, source_target_pairs={{1,9},{3,11},{9,17},{11,19},{13,5},{15,7},{17,25},{19,27},{21,13},... | collective-permute-start | bytes 6291464 | tf_op jit(solution)/shard_map/ppermute | solution.py:238
  4.5 3.5 %collective-permute-start = (bf16[1024,128]{1,0:T(8,128)(2,1)}, bf16[1024,128]{1,0:T(8,128)(2,1)S(1)}, u32[]{:S(2)}, u32[]{:S(2)}) collective-permute-start(bf16[1024,128]{1,0:T(8,128)(2,1)} %query_ref.5), channel_id=1, source_target_pairs={{1,5},{3,7},{4,12},{5,1},{6,14},{7,3},{8,0},{9,13},{10,2},{11,15},... | collective-permute-start | bytes 786440 | tf_op jit(solution)/shard_map/ppermute | solution.py:238
  7.9 6.0 %all_gather.3.refs_0_ = bf16[1024,128]{1,0:T(8,128)(2,1)S(1)} all-gather(bf16[256,128]{1,0:T(8,128)(2,1)} %param.5), channel_id=1, replica_groups=mesh['pb'=8,'ao'=4] {'ao'}, dimensions={0}, use_global_device_ids=true | all-gather | bytes 327680 | tf_op jit(solution)/shard_map/all_gather | solution.py:249
  13.9 1.9 %collective-permute-done.query_ref = bf16[1024,128]{1,0:T(8,128)(2,1)S(1)} collective-permute-done((bf16[1024,128]{1,0:T(8,128)(2,1)}, bf16[1024,128]{1,0:T(8,128)(2,1)S(1)}, u32[]{:S(2)}, u32[]{:S(2)}) %collective-permute-start) | collective-permute-done | bytes 262176 | tf_op jit(solution)/shard_map/ppermute | solution.py:238
  15.8 2.9 %collective-permute-start.1 = (bf16[1024,128]{1,0:T(8,128)(2,1)S(1)}, bf16[1024,128]{1,0:T(8,128)(2,1)S(1)}, u32[]{:S(2)}, u32[]{:S(2)}) collective-permute-start(bf16[1024,128]{1,0:T(8,128)(2,1)S(1)} %all_gather.3.refs_0_), channel_id=1, source_target_pairs={{1,4},{3,6},{4,13},{5,0},{6,15},{7,2},{8,1},{9,12},{10,3},{11,14},... | collective-permute-start | bytes 786440 | tf_op jit(solution)/shard_map/ppermute | solution.py:238
  18.7 0.1 pad_add_fusion.place_ref
  18.8 0.0 copy-start.1
  18.8 0.7 copy-done.1
  19.5 0.0 copy-start
  19.5 0.0 copy-start.2
  19.5 5.1 %kern.5.refs_2_ = bf16[1024,1024]{1,0:T(8,128)(2,1)S(1)} custom-call(s32[2]{0:T(128)S(1)} %pad_add_fusion.place_ref, s32[8,5]{1,0:T(8,128)S(1)} %copy-done.1, bf16[1024,128]{1,0:T(8,128)(2,1)S(1)} %collective-permute-done.query_ref, bf16[1024,128]{1,0:T(8,128)(2,1)S(1)} %all_gather.3.refs_0_, bf16[1024,1024]{1,0:T(8,128)(2,1)} %refs_2_.1), custom_call_target="tpu_custom_call" | custom-call | flops 1048576 | bytes 65536 | tf_op jit(solution)/shard_map/kern/pallas_call | solution.py:131
  24.6 0.0 copy-done
  24.6 0.0 copy-done.2
  24.6 5.7 %kern.6 = (bf16[1024,1024]{1,0:T(8,128)(2,1)S(1)}, bf16[1024,512]{1,0:T(8,128)(2,1)S(1)}, bf16[1024,512]{1,0:T(8,128)(2,1)S(1)}) custom-call(s32[2]{0:T(128)S(1)} %pad_add_fusion.place_ref, s32[8,5]{1,0:T(8,128)S(1)} %copy-done.2, bf16[1024,128]{1,0:T(8,128)(2,1)S(1)} %copy-done, bf16[1024,128]{1,0:T(8,128)(2,1)S(1)} %all_gather.3.refs_0_, ...), custom_call_target="tpu_custom_call" | custom-call | flops 1048576 | bytes 65536 | tf_op jit(solution)/shard_map/kern/pallas_call | solution.py:131
  30.4 0.0 collective-permute-done.1.refs_0_
  30.4 2.6 %kern.7.refs_0_ = bf16[1024,1024]{1,0:T(8,128)(2,1)S(1)} custom-call(s32[2]{0:T(128)S(1)} %pad_add_fusion.place_ref, s32[8,5]{1,0:T(8,128)S(1)} %copy-done.2, bf16[1024,128]{1,0:T(8,128)(2,1)S(1)} %collective-permute-done.query_ref, bf16[1024,128]{1,0:T(8,128)(2,1)S(1)} %collective-permute-done.1.refs_0_), custom_call_target="tpu_custom_call" | custom-call | flops 1048576 | bytes 65536 | tf_op jit(solution)/shard_map/kern/pallas_call | solution.py:131
  33.0 4.8 %collective-permute-start.8 = (bf16[1024,512]{1,0:T(8,128)(2,1)S(1)}, bf16[1024,512]{1,0:T(8,128)(2,1)S(1)}, u32[]{:S(2)}, u32[]{:S(2)}) collective-permute-start(bf16[1024,512]{1,0:T(8,128)(2,1)S(1)} %get-tuple-element.32), channel_id=1, source_target_pairs={{4,12},{6,14},{8,0},{10,2},{12,20},{14,22},{16,8},{18,10},{20,28},... | collective-permute-start | bytes 3145736 | tf_op jit(solution)/shard_map/ppermute | solution.py:238
  37.9 0.0 collective-permute-done.2.refs_1_
  37.9 1.8 %scores.3 = bf16[1024,512]{1,0:T(8,128)(2,1)S(1)} custom-call(bf16[1024,1024]{1,0:T(8,128)(2,1)S(1)} %kern.7.refs_0_, bf16[1024,1024]{1,0:T(8,128)(2,1)S(1)} %collective-permute-done.2.refs_1_, bf16[1024,1024]{1,0:T(8,128)(2,1)S(1)} %kern.5.refs_2_), custom_call_target="tpu_custom_call" | custom-call | flops 1048576 | bytes 65536 | tf_op jit(solution)/shard_map/scores/pallas_call | solution.py:174
  39.6 1.9 %collective-permute-start.9 = (bf16[1024,512]{1,0:T(8,128)(2,1)S(1)}, bf16[1024,512]{1,0:T(8,128)(2,1)S(1)}, u32[]{:S(2)}, u32[]{:S(2)}) collective-permute-start(bf16[1024,512]{1,0:T(8,128)(2,1)S(1)} %scores.3), channel_id=1, source_target_pairs={{0,8},{1,5},{2,10},{3,7},{5,1},{7,3},{8,16},{9,13},{10,18},{11,15}... | collective-permute-start | bytes 3145736 | tf_op jit(solution)/shard_map/ppermute | solution.py:238
  41.6 0.0 collective-permute-done.3.refs_3_
  41.6 3.9 %collective-permute-start.6 = (bf16[1024,512]{1,0:T(8,128)(2,1)S(1)}, bf16[1024,512]{1,0:T(8,128)(2,1)S(1)}, u32[]{:S(2)}, u32[]{:S(2)}) collective-permute-start(bf16[1024,512]{1,0:T(8,128)(2,1)S(1)} %get-tuple-element.29), channel_id=1, source_target_pairs={{4,12},{6,14},{8,0},{10,2},{12,20},{14,22},{16,8},{18,10},{20,28},... | collective-permute-start | bytes 3145736 | tf_op jit(solution)/shard_map/ppermute | solution.py:238
  45.5 1.8 %scores.2 = bf16[1024,512]{1,0:T(8,128)(2,1)S(1)} custom-call(bf16[1024,1024]{1,0:T(8,128)(2,1)S(1)} %kern.7.refs_0_, bf16[1024,1024]{1,0:T(8,128)(2,1)S(1)} %collective-permute-done.2.refs_1_, bf16[1024,1024]{1,0:T(8,128)(2,1)S(1)} %kern.5.refs_2_), custom_call_target="tpu_custom_call" | custom-call | flops 1048576 | bytes 65536 | tf_op jit(solution)/shard_map/scores/pallas_call | solution.py:174
  47.3 2.0 %collective-permute-start.7 = (bf16[1024,512]{1,0:T(8,128)(2,1)S(1)}, bf16[1024,512]{1,0:T(8,128)(2,1)S(1)}, u32[]{:S(2)}, u32[]{:S(2)}) collective-permute-start(bf16[1024,512]{1,0:T(8,128)(2,1)S(1)} %scores.2), channel_id=1, source_target_pairs={{0,8},{1,5},{2,10},{3,7},{5,1},{7,3},{8,16},{9,13},{10,18},{11,15}... | collective-permute-start | bytes 3145736 | tf_op jit(solution)/shard_map/ppermute | solution.py:238
  49.3 1.3 %collective-permute-start.4 = (bf16[1024,128]{1,0:T(8,128)(2,1)S(1)}, bf16[1024,128]{1,0:T(8,128)(2,1)S(1)}, u32[]{:S(2)}, u32[]{:S(2)}) collective-permute-start(bf16[1024,128]{1,0:T(8,128)(2,1)S(1)} %collective-permute-done.1.refs_0_), channel_id=1, source_target_pairs={{1,0},{3,2},{5,4},{7,6},{9,8},{11,10},{13,12},{15,14},{17,16},{19,... | collective-permute-start | bytes 786440 | tf_op jit(solution)/shard_map/ppermute | solution.py:238
  50.6 2.1 %collective-permute-done.4.refs_0_ = bf16[1024,128]{1,0:T(8,128)(2,1)S(1)} collective-permute-done((bf16[1024,128]{1,0:T(8,128)(2,1)S(1)}, bf16[1024,128]{1,0:T(8,128)(2,1)S(1)}, u32[]{:S(2)}, u32[]{:S(2)}) %collective-permute-start.4) | collective-permute-done | bytes 262176 | tf_op jit(solution)/shard_map/ppermute | solution.py:238
  52.7 0.8 %collective-permute-start.5 = (bf16[1024,128]{1,0:T(8,128)(2,1)S(1)}, bf16[1024,128]{1,0:T(8,128)(2,1)S(1)}, u32[]{:S(2)}, u32[]{:S(2)}) collective-permute-start(bf16[1024,128]{1,0:T(8,128)(2,1)S(1)} %all_gather.3.refs_0_), channel_id=1, source_target_pairs={{1,9},{3,11},{9,17},{11,19},{13,5},{15,7},{17,25},{19,27},{21,13},... | collective-permute-start | bytes 786440 | tf_op jit(solution)/shard_map/ppermute | solution.py:238
  53.6 5.3 %kern.8 = (f32[1024,1024]{1,0:T(8,128)S(1)}, bf16[1024,1024]{1,0:T(8,128)(2,1)S(1)}) custom-call(s32[2]{0:T(128)S(1)} %pad_add_fusion.place_ref, s32[8,5]{1,0:T(8,128)S(1)} %copy-done.2, bf16[1024,128]{1,0:T(8,128)(2,1)S(1)} %copy-done, bf16[1024,128]{1,0:T(8,128)(2,1)S(1)} %collective-permute-done.1.refs_0_, ...), custom_call_target="tpu_custom_call" | custom-call | flops 1048576 | bytes 65536 | tf_op jit(solution)/shard_map/kern/pallas_call | solution.py:131
  58.8 0.0 collective-permute-done.5.refs_1_
  58.9 2.6 %kern.9.kern_ref = bf16[1024,1024]{1,0:T(8,128)(2,1)S(1)} custom-call(s32[2]{0:T(128)S(1)} %pad_add_fusion.place_ref, s32[8,5]{1,0:T(8,128)S(1)} %copy-done.2, bf16[1024,128]{1,0:T(8,128)(2,1)S(1)} %copy-done, bf16[1024,128]{1,0:T(8,128)(2,1)S(1)} %collective-permute-done.4.refs_0_, bf16[1024,128]{1,0:T(8,128)(2,1)S(1)} %collective-permute-done.5.refs_1_), custom_call_target="tpu_custom_call" | custom-call | flops 1048576 | bytes 65536 | tf_op jit(solution)/shard_map/kern/pallas_call | solution.py:131
  61.5 0.0 collective-permute-done.8.far_0_ref
  61.5 0.0 collective-permute-done.9.part_ref
  61.5 2.9 %final.2.refs_0_ = bf16[1024,1024]{1,0:T(8,128)(2,1)} custom-call(s32[2]{0:T(128)S(1)} %pad_add_fusion.place_ref, bf16[1024,1024]{1,0:T(8,128)(2,1)S(1)} %kern.9.kern_ref, bf16[1024,512]{1,0:T(8,128)(2,1)S(1)} %collective-permute-done.8.far_0_ref, bf16[1024,1024]{1,0:T(8,128)(2,1)S(1)} %get-tuple-element.30.far_1_ref, ...), custom_call_target="tpu_custom_call" | custom-call | flops 1048576 | bytes 65536 | tf_op jit(solution)/shard_map/final/pallas_call | solution.py:208
  64.4 0.0 collective-permute-done.6.far_0_ref
  64.4 6.0 %collective-permute-done.7.part_ref = bf16[1024,512]{1,0:T(8,128)(2,1)S(1)} collective-permute-done((bf16[1024,512]{1,0:T(8,128)(2,1)S(1)}, bf16[1024,512]{1,0:T(8,128)(2,1)S(1)}, u32[]{:S(2)}, u32[]{:S(2)}) %collective-permute-start.7) | collective-permute-done | bytes 1048608 | tf_op jit(solution)/shard_map/ppermute | solution.py:238
  70.4 2.9 %final.3 = bf16[1024,1024]{1,0:T(8,128)(2,1)} custom-call(s32[2]{0:T(128)S(1)} %pad_add_fusion.place_ref, bf16[1024,1024]{1,0:T(8,128)(2,1)S(1)} %kern.9.kern_ref, bf16[1024,512]{1,0:T(8,128)(2,1)S(1)} %collective-permute-done.6.far_0_ref, bf16[1024,1024]{1,0:T(8,128)(2,1)S(1)} %get-tuple-element.30.far_1_ref, ...), custom_call_target="tpu_custom_call", output_to_operand_aliasing={{}: (6, {})} | custom-call | flops 1048576 | bytes 65536 | tf_op jit(solution)/shard_map/final/pallas_call | solution.py:208
Async XLA Ops:
  0.0 37.9 %collective-permute-start.2 = (bf16[1024,1024]{1,0:T(8,128)(2,1)}, bf16[1024,1024]{1,0:T(8,128)(2,1)S(1)}, u32[]{:S(2)}, u32[]{:S(2)}) collective-permute-start(bf16[1024,1024]{1,0:T(8,128)(2,1)} %refs_2_.1), channel_id=1, source_target_pairs={{0,4},{2,6},{4,0},{5,13},{6,2},{7,15},{8,12},{9,1},{10,14},{11,3},... | collective-permute-start | bytes 6291464 | tf_op jit(solution)/shard_map/ppermute | solution.py:238
  2.4 39.1 %collective-permute-start.3 = (bf16[1024,1024]{1,0:T(8,128)(2,1)}, bf16[1024,1024]{1,0:T(8,128)(2,1)}, u32[]{:S(2)}, u32[]{:S(2)}) collective-permute-start(bf16[1024,1024]{1,0:T(8,128)(2,1)} %refs_2_.1), channel_id=1, source_target_pairs={{1,9},{3,11},{9,17},{11,19},{13,5},{15,7},{17,25},{19,27},{21,13},... | collective-permute-start | bytes 6291464 | tf_op jit(solution)/shard_map/ppermute | solution.py:238
  4.5 11.3 %collective-permute-start = (bf16[1024,128]{1,0:T(8,128)(2,1)}, bf16[1024,128]{1,0:T(8,128)(2,1)S(1)}, u32[]{:S(2)}, u32[]{:S(2)}) collective-permute-start(bf16[1024,128]{1,0:T(8,128)(2,1)} %query_ref.5), channel_id=1, source_target_pairs={{1,5},{3,7},{4,12},{5,1},{6,14},{7,3},{8,0},{9,13},{10,2},{11,15},... | collective-permute-start | bytes 786440 | tf_op jit(solution)/shard_map/ppermute | solution.py:238
  15.8 14.6 %collective-permute-start.1 = (bf16[1024,128]{1,0:T(8,128)(2,1)S(1)}, bf16[1024,128]{1,0:T(8,128)(2,1)S(1)}, u32[]{:S(2)}, u32[]{:S(2)}) collective-permute-start(bf16[1024,128]{1,0:T(8,128)(2,1)S(1)} %all_gather.3.refs_0_), channel_id=1, source_target_pairs={{1,4},{3,6},{4,13},{5,0},{6,15},{7,2},{8,1},{9,12},{10,3},{11,14},... | collective-permute-start | bytes 786440 | tf_op jit(solution)/shard_map/ppermute | solution.py:238
  18.8 0.7 copy-start.1
  19.5 5.1 %copy-start = (bf16[1024,128]{1,0:T(8,128)(2,1)S(1)}, bf16[1024,128]{1,0:T(8,128)(2,1)}, u32[]{:S(2)}) copy-start(bf16[1024,128]{1,0:T(8,128)(2,1)} %query_ref.5) | copy-start | bytes 786436
  19.5 5.1 %copy-start.2 = (s32[8,5]{1,0:T(8,128)S(1)}, s32[8,5]{1,0:T(8,128)}, u32[]{:S(2)}) copy-start(s32[8,5]{1,0:T(8,128)} %pattern_ref.9) | copy-start | bytes 484
  33.0 28.5 %collective-permute-start.8 = (bf16[1024,512]{1,0:T(8,128)(2,1)S(1)}, bf16[1024,512]{1,0:T(8,128)(2,1)S(1)}, u32[]{:S(2)}, u32[]{:S(2)}) collective-permute-start(bf16[1024,512]{1,0:T(8,128)(2,1)S(1)} %get-tuple-element.32), channel_id=1, source_target_pairs={{4,12},{6,14},{8,0},{10,2},{12,20},{14,22},{16,8},{18,10},{20,28},... | collective-permute-start | bytes 3145736 | tf_op jit(solution)/shard_map/ppermute | solution.py:238
  39.6 21.9 %collective-permute-start.9 = (bf16[1024,512]{1,0:T(8,128)(2,1)S(1)}, bf16[1024,512]{1,0:T(8,128)(2,1)S(1)}, u32[]{:S(2)}, u32[]{:S(2)}) collective-permute-start(bf16[1024,512]{1,0:T(8,128)(2,1)S(1)} %scores.3), channel_id=1, source_target_pairs={{0,8},{1,5},{2,10},{3,7},{5,1},{7,3},{8,16},{9,13},{10,18},{11,15}... | collective-permute-start | bytes 3145736 | tf_op jit(solution)/shard_map/ppermute | solution.py:238
  41.6 22.8 %collective-permute-start.6 = (bf16[1024,512]{1,0:T(8,128)(2,1)S(1)}, bf16[1024,512]{1,0:T(8,128)(2,1)S(1)}, u32[]{:S(2)}, u32[]{:S(2)}) collective-permute-start(bf16[1024,512]{1,0:T(8,128)(2,1)S(1)} %get-tuple-element.29), channel_id=1, source_target_pairs={{4,12},{6,14},{8,0},{10,2},{12,20},{14,22},{16,8},{18,10},{20,28},... | collective-permute-start | bytes 3145736 | tf_op jit(solution)/shard_map/ppermute | solution.py:238
  47.3 23.1 %collective-permute-start.7 = (bf16[1024,512]{1,0:T(8,128)(2,1)S(1)}, bf16[1024,512]{1,0:T(8,128)(2,1)S(1)}, u32[]{:S(2)}, u32[]{:S(2)}) collective-permute-start(bf16[1024,512]{1,0:T(8,128)(2,1)S(1)} %scores.2), channel_id=1, source_target_pairs={{0,8},{1,5},{2,10},{3,7},{5,1},{7,3},{8,16},{9,13},{10,18},{11,15}... | collective-permute-start | bytes 3145736 | tf_op jit(solution)/shard_map/ppermute | solution.py:238
  49.3 3.4 %collective-permute-start.4 = (bf16[1024,128]{1,0:T(8,128)(2,1)S(1)}, bf16[1024,128]{1,0:T(8,128)(2,1)S(1)}, u32[]{:S(2)}, u32[]{:S(2)}) collective-permute-start(bf16[1024,128]{1,0:T(8,128)(2,1)S(1)} %collective-permute-done.1.refs_0_), channel_id=1, source_target_pairs={{1,0},{3,2},{5,4},{7,6},{9,8},{11,10},{13,12},{15,14},{17,16},{19,... | collective-permute-start | bytes 786440 | tf_op jit(solution)/shard_map/ppermute | solution.py:238
  52.7 6.2 %collective-permute-start.5 = (bf16[1024,128]{1,0:T(8,128)(2,1)S(1)}, bf16[1024,128]{1,0:T(8,128)(2,1)S(1)}, u32[]{:S(2)}, u32[]{:S(2)}) collective-permute-start(bf16[1024,128]{1,0:T(8,128)(2,1)S(1)} %all_gather.3.refs_0_), channel_id=1, source_target_pairs={{1,9},{3,11},{9,17},{11,19},{13,5},{15,7},{17,25},{19,27},{21,13},... | collective-permute-start | bytes 786440 | tf_op jit(solution)/shard_map/ppermute | solution.py:238
